TPU v7x, 256 devices: a whole 4x4x8 slice. The times are simulated.
256 devices in a mesh: chan: 16 (over y, x), win: 16 (over z, core).
Axes of the slice: x: 4, y: 4, z: 8, core: 2. Of those that a mesh axis runs over, the one named last changes fastest.
Arguments:
- spectra: float32 [2, 1024, 32, 2048], P(None, 'win', None, 'chan'), may hold values from -180 to 180
- quality_mask: int32 [1024, 2048], P('win', 'chan'), may hold values 0 or 1
Outputs:
- stacked: float32 [32, 2, 2048, 2048], P('win', None, 'chan')
All inputs are finite; a program needn't handle non-finite values. No bound on the sum of `quality_mask` on one device may be relied on, other than what follows from the above.
Results may differ from a plain program's by a relative error of at most 0.0028.
Values may be sent and summed in bfloat16 or wider, within the bound.
A program may use at most 64 MiB of HBM per device.

v0:
```python
import math

import jax
import jax.numpy as jnp
from jax import lax
from jax.sharding import PartitionSpec as P


def from_behind(shard, axis, by):
    devices = lax.axis_size(axis)
    return lax.ppermute(shard, axis, [(i, (i + by) % devices) for i in range(devices)])


def body(spectra, quality_mask):
    rms_level = jnp.sqrt(jnp.mean(spectra * spectra, axis=(0, 2)) + 1e-06)
    factor = quality_mask.astype(jnp.float32) / rms_level
    whitened = (spectra * factor[None, :, None, :]).astype(jnp.bfloat16)
    spread = lax.all_to_all(whitened, "win", split_axis=2, concat_axis=1, tiled=True)
    paired = jnp.stack([spread, jnp.stack([spread[1], -spread[0]])])
    inv_root = 1.0 / math.sqrt(spread.shape[1])
    cycle_size = lax.axis_size("chan")
    cycle_index = lax.axis_index("chan")
    block_width = spread.shape[3]
    bins_dev = spread.shape[2]

    def cross_block(held_block):
        return (
            jnp.einsum("kpwfc,pwfd->fkcd", paired, held_block, preferred_element_type=jnp.float32)
            * inv_root
        )

    def place_block(stack_now, held_block, source):
        offset_col = jnp.mod(source, cycle_size) * block_width
        return lax.dynamic_update_slice_in_dim(stack_now, cross_block(held_block), offset_col, 3)

    zero_stack = jnp.zeros((bins_dev, 2, block_width, block_width * cycle_size), jnp.float32)
    stacked = place_block(zero_stack, spread, cycle_index)

    def cycle_turn(step_index, loop_state):
        stack_now, held_block = loop_state
        held_block = from_behind(held_block, "chan", 1)
        return (place_block(stack_now, held_block, cycle_index - step_index), held_block)

    stacked, held_block = lax.fori_loop(1, cycle_size, cycle_turn, (stacked, spread))
    return stacked


def solution(mesh):
    placed = (P(None, "win", None, "chan"), P("win", "chan"))
    return jax.shard_map(
        body, mesh=mesh, in_specs=placed, out_specs=P("win", None, "chan", None), check_vma=False
    )
```

profile of v0, /device:TPU:0, one launch (start us, length us, event | category | flops | bytes accessed | tf_op | source)
XLA Modules:
  0.0 443.3 jit_solution(3210222252957882018)
XLA Ops:
  0.0 2.1 multiply_reduce_fusion
  2.2 2.2 fusion.3
  4.4 6.8 %all-to-all-start = ((bf16[2,64,32,128]{3,1,0,2:T(8,128)(2,1)}), bf16[2,64,32,128]{3,1,0,2:T(8,128)(2,1)S(1)}, u32[]{:S(2)}, u32[]{:S(2)}) async-start(bf16[2,64,32,128]{3,1,0,2:T(8,128)(2,1)} %fusion.3), calls=%async_computation | async-start | bytes 2097152 | tf_op jit(solution)/shard_map/all_to_all | solution.py:18
  11.3 26.6 %all-to-all-done = bf16[2,64,32,128]{3,1,0,2:T(8,128)(2,1)S(1)} async-done(((bf16[2,64,32,128]{3,1,0,2:T(8,128)(2,1)}), bf16[2,64,32,128]{3,1,0,2:T(8,128)(2,1)S(1)}, u32[]{:S(2)}, u32[]{:S(2)}) %all-to-all-start) | async-done | bytes 1048608 | tf_op jit(solution)/shard_map/all_to_all | solution.py:18
  38.0 1.1 copy.27
  39.6 1.0 copy.25
  43.9 2.0 copy-done.1
  45.9 397.4 %while.17 = (s32[]{:T(128)}, f32[2,2,128,2048]{3,2,1,0:T(8,128)}, bf16[2,1024,2,128]{3,1,0,2:T(8,128)(2,1)}, bf16[2,2,1024,2,128]{2,4,1,0,3:T(8,128)(2,1)S(1)}, ...) while((s32[]{:T(128)}, f32[2,2,128,2048]{3,2,1,0:T(8,128)}, ...), condition=%wide.region_2.3_spmd, body=%wide.region_1.2_spmd.sunk | while | flops 268501024 | bytes 9699648 | solution.py:44
  45.9 1.5 collective-permute-start
  47.4 27.2 %collective-permute-done = bf16[2,1024,2,128]{3,1,0,2:T(8,128)(2,1)S(1)} collective-permute-done((bf16[2,1024,2,128]{3,1,0,2:T(8,128)(2,1)}, bf16[2,1024,2,128]{3,1,0,2:T(8,128)(2,1)S(1)}, u32[]{:S(2)}, u32[]{:S(2)}) %collective-permute-start) | collective-permute-done | bytes 1048608 | tf_op jit(solution)/shard_map/while/body/eval_jaxpr/ppermute | solution.py:11
  74.6 1.0 copy.47
  75.6 1.4 fusion.14
  77.0 29.3 %collective-permute-done = bf16[2,1024,2,128]{3,1,0,2:T(8,128)(2,1)S(1)} collective-permute-done((bf16[2,1024,2,128]{3,1,0,2:T(8,128)(2,1)}, bf16[2,1024,2,128]{3,1,0,2:T(8,128)(2,1)S(1)}, u32[]{:S(2)}, u32[]{:S(2)}) %collective-permute-start) | collective-permute-done | bytes 1048608 | tf_op jit(solution)/shard_map/while/body/eval_jaxpr/ppermute | solution.py:11
  107.2 1.4 fusion.14
  108.6 28.4 %collective-permute-done = bf16[2,1024,2,128]{3,1,0,2:T(8,128)(2,1)S(1)} collective-permute-done((bf16[2,1024,2,128]{3,1,0,2:T(8,128)(2,1)}, bf16[2,1024,2,128]{3,1,0,2:T(8,128)(2,1)S(1)}, u32[]{:S(2)}, u32[]{:S(2)}) %collective-permute-start) | collective-permute-done | bytes 1048608 | tf_op jit(solution)/shard_map/while/body/eval_jaxpr/ppermute | solution.py:11
  137.0 1.0 copy.47
  138.0 1.4 fusion.14
  139.4 27.5 %collective-permute-done = bf16[2,1024,2,128]{3,1,0,2:T(8,128)(2,1)S(1)} collective-permute-done((bf16[2,1024,2,128]{3,1,0,2:T(8,128)(2,1)}, bf16[2,1024,2,128]{3,1,0,2:T(8,128)(2,1)S(1)}, u32[]{:S(2)}, u32[]{:S(2)}) %collective-permute-start) | collective-permute-done | bytes 1048608 | tf_op jit(solution)/shard_map/while/body/eval_jaxpr/ppermute | solution.py:11
  166.9 1.0 copy.47
  167.9 1.4 fusion.14
  169.3 26.6 %collective-permute-done = bf16[2,1024,2,128]{3,1,0,2:T(8,128)(2,1)S(1)} collective-permute-done((bf16[2,1024,2,128]{3,1,0,2:T(8,128)(2,1)}, bf16[2,1024,2,128]{3,1,0,2:T(8,128)(2,1)S(1)}, u32[]{:S(2)}, u32[]{:S(2)}) %collective-permute-start) | collective-permute-done | bytes 1048608 | tf_op jit(solution)/shard_map/while/body/eval_jaxpr/ppermute | solution.py:11
  195.9 1.0 copy.47
  196.8 1.4 fusion.14
  198.2 25.7 %collective-permute-done = bf16[2,1024,2,128]{3,1,0,2:T(8,128)(2,1)S(1)} collective-permute-done((bf16[2,1024,2,128]{3,1,0,2:T(8,128)(2,1)}, bf16[2,1024,2,128]{3,1,0,2:T(8,128)(2,1)S(1)}, u32[]{:S(2)}, u32[]{:S(2)}) %collective-permute-start) | collective-permute-done | bytes 1048608 | tf_op jit(solution)/shard_map/while/body/eval_jaxpr/ppermute | solution.py:11
  223.9 1.0 copy.47
  224.9 1.4 fusion.14
  226.3 24.8 %collective-permute-done = bf16[2,1024,2,128]{3,1,0,2:T(8,128)(2,1)S(1)} collective-permute-done((bf16[2,1024,2,128]{3,1,0,2:T(8,128)(2,1)}, bf16[2,1024,2,128]{3,1,0,2:T(8,128)(2,1)S(1)}, u32[]{:S(2)}, u32[]{:S(2)}) %collective-permute-start) | collective-permute-done | bytes 1048608 | tf_op jit(solution)/shard_map/while/body/eval_jaxpr/ppermute | solution.py:11
  252.0 1.4 fusion.14
  253.4 23.8 %collective-permute-done = bf16[2,1024,2,128]{3,1,0,2:T(8,128)(2,1)S(1)} collective-permute-done((bf16[2,1024,2,128]{3,1,0,2:T(8,128)(2,1)}, bf16[2,1024,2,128]{3,1,0,2:T(8,128)(2,1)S(1)}, u32[]{:S(2)}, u32[]{:S(2)}) %collective-permute-start) | collective-permute-done | bytes 1048608 | tf_op jit(solution)/shard_map/while/body/eval_jaxpr/ppermute | solution.py:11
  278.2 1.4 fusion.14
  279.6 22.9 %collective-permute-done = bf16[2,1024,2,128]{3,1,0,2:T(8,128)(2,1)S(1)} collective-permute-done((bf16[2,1024,2,128]{3,1,0,2:T(8,128)(2,1)}, bf16[2,1024,2,128]{3,1,0,2:T(8,128)(2,1)S(1)}, u32[]{:S(2)}, u32[]{:S(2)}) %collective-permute-start) | collective-permute-done | bytes 1048608 | tf_op jit(solution)/shard_map/while/body/eval_jaxpr/ppermute | solution.py:11
  303.5 1.4 fusion.14
  304.9 22.0 %collective-permute-done = bf16[2,1024,2,128]{3,1,0,2:T(8,128)(2,1)S(1)} collective-permute-done((bf16[2,1024,2,128]{3,1,0,2:T(8,128)(2,1)}, bf16[2,1024,2,128]{3,1,0,2:T(8,128)(2,1)S(1)}, u32[]{:S(2)}, u32[]{:S(2)}) %collective-permute-start) | collective-permute-done | bytes 1048608 | tf_op jit(solution)/shard_map/while/body/eval_jaxpr/ppermute | solution.py:11
  326.9 1.0 copy.47
  327.8 1.4 fusion.14
  329.2 21.1 %collective-permute-done = bf16[2,1024,2,128]{3,1,0,2:T(8,128)(2,1)S(1)} collective-permute-done((bf16[2,1024,2,128]{3,1,0,2:T(8,128)(2,1)}, bf16[2,1024,2,128]{3,1,0,2:T(8,128)(2,1)S(1)}, u32[]{:S(2)}, u32[]{:S(2)}) %collective-permute-start) | collective-permute-done | bytes 1048608 | tf_op jit(solution)/shard_map/while/body/eval_jaxpr/ppermute | solution.py:11
  350.3 1.0 copy.47
  351.3 1.4 fusion.14
  352.7 21.0 %collective-permute-done = bf16[2,1024,2,128]{3,1,0,2:T(8,128)(2,1)S(1)} collective-permute-done((bf16[2,1024,2,128]{3,1,0,2:T(8,128)(2,1)}, bf16[2,1024,2,128]{3,1,0,2:T(8,128)(2,1)S(1)}, u32[]{:S(2)}, u32[]{:S(2)}) %collective-permute-start) | collective-permute-done | bytes 1048608 | tf_op jit(solution)/shard_map/while/body/eval_jaxpr/ppermute | solution.py:11
  373.6 1.0 copy.47
  374.6 1.4 fusion.14
  376.0 21.0 %collective-permute-done = bf16[2,1024,2,128]{3,1,0,2:T(8,128)(2,1)S(1)} collective-permute-done((bf16[2,1024,2,128]{3,1,0,2:T(8,128)(2,1)}, bf16[2,1024,2,128]{3,1,0,2:T(8,128)(2,1)S(1)}, u32[]{:S(2)}, u32[]{:S(2)}) %collective-permute-start) | collective-permute-done | bytes 1048608 | tf_op jit(solution)/shard_map/while/body/eval_jaxpr/ppermute | solution.py:11
  397.9 1.4 fusion.14
  399.3 21.0 %collective-permute-done = bf16[2,1024,2,128]{3,1,0,2:T(8,128)(2,1)S(1)} collective-permute-done((bf16[2,1024,2,128]{3,1,0,2:T(8,128)(2,1)}, bf16[2,1024,2,128]{3,1,0,2:T(8,128)(2,1)S(1)}, u32[]{:S(2)}, u32[]{:S(2)}) %collective-permute-start) | collective-permute-done | bytes 1048608 | tf_op jit(solution)/shard_map/while/body/eval_jaxpr/ppermute | solution.py:11
  420.3 1.0 copy.47
  421.2 1.4 fusion.14
  422.6 18.3 %collective-permute-done = bf16[2,1024,2,128]{3,1,0,2:T(8,128)(2,1)S(1)} collective-permute-done((bf16[2,1024,2,128]{3,1,0,2:T(8,128)(2,1)}, bf16[2,1024,2,128]{3,1,0,2:T(8,128)(2,1)S(1)}, u32[]{:S(2)}, u32[]{:S(2)}) %collective-permute-start) | collective-permute-done | bytes 1048608 | tf_op jit(solution)/shard_map/while/body/eval_jaxpr/ppermute | solution.py:11
  441.9 1.4 fusion.14
  (41 shorter events, 9.8 us)
Async XLA Ops:
  0.0 2.2 copy-start
  0.0 2.1 copy-start.4
  4.4 33.5 %all-to-all-start = ((bf16[2,64,32,128]{3,1,0,2:T(8,128)(2,1)}), bf16[2,64,32,128]{3,1,0,2:T(8,128)(2,1)S(1)}, u32[]{:S(2)}, u32[]{:S(2)}) async-start(bf16[2,64,32,128]{3,1,0,2:T(8,128)(2,1)} %fusion.3), calls=%async_computation | async-start | bytes 2097152 | tf_op jit(solution)/shard_map/all_to_all | solution.py:18
  40.6 1.0 copy-start.2
  41.9 1.2 copy-start.3
  43.9 2.0 copy-start.1
  45.9 28.7 %collective-permute-start = (bf16[2,1024,2,128]{3,1,0,2:T(8,128)(2,1)}, bf16[2,1024,2,128]{3,1,0,2:T(8,128)(2,1)S(1)}, u32[]{:S(2)}, u32[]{:S(2)}) collective-permute-start(bf16[2,1024,2,128]{3,1,0,2:T(8,128)(2,1)} %get-tuple-element.195), channel_id=1, source_target_pairs={{0,16},{16,32},{32,48},{48,64},{64,80},{80,96},{96,112},{112,128},... | collective-permute-start | bytes 3145736 | tf_op jit(solution)/shard_map/while/body/eval_jaxpr/ppermute | solution.py:11
  77.0 29.3 %collective-permute-start = (bf16[2,1024,2,128]{3,1,0,2:T(8,128)(2,1)}, bf16[2,1024,2,128]{3,1,0,2:T(8,128)(2,1)S(1)}, u32[]{:S(2)}, u32[]{:S(2)}) collective-permute-start(bf16[2,1024,2,128]{3,1,0,2:T(8,128)(2,1)} %get-tuple-element.195), channel_id=1, source_target_pairs={{0,16},{16,32},{32,48},{48,64},{64,80},{80,96},{96,112},{112,128},... | collective-permute-start | bytes 3145736 | tf_op jit(solution)/shard_map/while/body/eval_jaxpr/ppermute | solution.py:11
  108.6 28.4 %collective-permute-start = (bf16[2,1024,2,128]{3,1,0,2:T(8,128)(2,1)}, bf16[2,1024,2,128]{3,1,0,2:T(8,128)(2,1)S(1)}, u32[]{:S(2)}, u32[]{:S(2)}) collective-permute-start(bf16[2,1024,2,128]{3,1,0,2:T(8,128)(2,1)} %get-tuple-element.195), channel_id=1, source_target_pairs={{0,16},{16,32},{32,48},{48,64},{64,80},{80,96},{96,112},{112,128},... | collective-permute-start | bytes 3145736 | tf_op jit(solution)/shard_map/while/body/eval_jaxpr/ppermute | solution.py:11
  139.4 27.5 %collective-permute-start = (bf16[2,1024,2,128]{3,1,0,2:T(8,128)(2,1)}, bf16[2,1024,2,128]{3,1,0,2:T(8,128)(2,1)S(1)}, u32[]{:S(2)}, u32[]{:S(2)}) collective-permute-start(bf16[2,1024,2,128]{3,1,0,2:T(8,128)(2,1)} %get-tuple-element.195), channel_id=1, source_target_pairs={{0,16},{16,32},{32,48},{48,64},{64,80},{80,96},{96,112},{112,128},... | collective-permute-start | bytes 3145736 | tf_op jit(solution)/shard_map/while/body/eval_jaxpr/ppermute | solution.py:11
  169.3 26.6 %collective-permute-start = (bf16[2,1024,2,128]{3,1,0,2:T(8,128)(2,1)}, bf16[2,1024,2,128]{3,1,0,2:T(8,128)(2,1)S(1)}, u32[]{:S(2)}, u32[]{:S(2)}) collective-permute-start(bf16[2,1024,2,128]{3,1,0,2:T(8,128)(2,1)} %get-tuple-element.195), channel_id=1, source_target_pairs={{0,16},{16,32},{32,48},{48,64},{64,80},{80,96},{96,112},{112,128},... | collective-permute-start | bytes 3145736 | tf_op jit(solution)/shard_map/while/body/eval_jaxpr/ppermute | solution.py:11
  198.2 25.7 %collective-permute-start = (bf16[2,1024,2,128]{3,1,0,2:T(8,128)(2,1)}, bf16[2,1024,2,128]{3,1,0,2:T(8,128)(2,1)S(1)}, u32[]{:S(2)}, u32[]{:S(2)}) collective-permute-start(bf16[2,1024,2,128]{3,1,0,2:T(8,128)(2,1)} %get-tuple-element.195), channel_id=1, source_target_pairs={{0,16},{16,32},{32,48},{48,64},{64,80},{80,96},{96,112},{112,128},... | collective-permute-start | bytes 3145736 | tf_op jit(solution)/shard_map/while/body/eval_jaxpr/ppermute | solution.py:11
  226.3 24.8 %collective-permute-start = (bf16[2,1024,2,128]{3,1,0,2:T(8,128)(2,1)}, bf16[2,1024,2,128]{3,1,0,2:T(8,128)(2,1)S(1)}, u32[]{:S(2)}, u32[]{:S(2)}) collective-permute-start(bf16[2,1024,2,128]{3,1,0,2:T(8,128)(2,1)} %get-tuple-element.195), channel_id=1, source_target_pairs={{0,16},{16,32},{32,48},{48,64},{64,80},{80,96},{96,112},{112,128},... | collective-permute-start | bytes 3145736 | tf_op jit(solution)/shard_map/while/body/eval_jaxpr/ppermute | solution.py:11
  253.4 23.8 %collective-permute-start = (bf16[2,1024,2,128]{3,1,0,2:T(8,128)(2,1)}, bf16[2,1024,2,128]{3,1,0,2:T(8,128)(2,1)S(1)}, u32[]{:S(2)}, u32[]{:S(2)}) collective-permute-start(bf16[2,1024,2,128]{3,1,0,2:T(8,128)(2,1)} %get-tuple-element.195), channel_id=1, source_target_pairs={{0,16},{16,32},{32,48},{48,64},{64,80},{80,96},{96,112},{112,128},... | collective-permute-start | bytes 3145736 | tf_op jit(solution)/shard_map/while/body/eval_jaxpr/ppermute | solution.py:11
  279.6 22.9 %collective-permute-start = (bf16[2,1024,2,128]{3,1,0,2:T(8,128)(2,1)}, bf16[2,1024,2,128]{3,1,0,2:T(8,128)(2,1)S(1)}, u32[]{:S(2)}, u32[]{:S(2)}) collective-permute-start(bf16[2,1024,2,128]{3,1,0,2:T(8,128)(2,1)} %get-tuple-element.195), channel_id=1, source_target_pairs={{0,16},{16,32},{32,48},{48,64},{64,80},{80,96},{96,112},{112,128},... | collective-permute-start | bytes 3145736 | tf_op jit(solution)/shard_map/while/body/eval_jaxpr/ppermute | solution.py:11
  304.9 22.0 %collective-permute-start = (bf16[2,1024,2,128]{3,1,0,2:T(8,128)(2,1)}, bf16[2,1024,2,128]{3,1,0,2:T(8,128)(2,1)S(1)}, u32[]{:S(2)}, u32[]{:S(2)}) collective-permute-start(bf16[2,1024,2,128]{3,1,0,2:T(8,128)(2,1)} %get-tuple-element.195), channel_id=1, source_target_pairs={{0,16},{16,32},{32,48},{48,64},{64,80},{80,96},{96,112},{112,128},... | collective-permute-start | bytes 3145736 | tf_op jit(solution)/shard_map/while/body/eval_jaxpr/ppermute | solution.py:11
  329.2 21.1 %collective-permute-start = (bf16[2,1024,2,128]{3,1,0,2:T(8,128)(2,1)}, bf16[2,1024,2,128]{3,1,0,2:T(8,128)(2,1)S(1)}, u32[]{:S(2)}, u32[]{:S(2)}) collective-permute-start(bf16[2,1024,2,128]{3,1,0,2:T(8,128)(2,1)} %get-tuple-element.195), channel_id=1, source_target_pairs={{0,16},{16,32},{32,48},{48,64},{64,80},{80,96},{96,112},{112,128},... | collective-permute-start | bytes 3145736 | tf_op jit(solution)/shard_map/while/body/eval_jaxpr/ppermute | solution.py:11
  352.7 21.0 %collective-permute-start = (bf16[2,1024,2,128]{3,1,0,2:T(8,128)(2,1)}, bf16[2,1024,2,128]{3,1,0,2:T(8,128)(2,1)S(1)}, u32[]{:S(2)}, u32[]{:S(2)}) collective-permute-start(bf16[2,1024,2,128]{3,1,0,2:T(8,128)(2,1)} %get-tuple-element.195), channel_id=1, source_target_pairs={{0,16},{16,32},{32,48},{48,64},{64,80},{80,96},{96,112},{112,128},... | collective-permute-start | bytes 3145736 | tf_op jit(solution)/shard_map/while/body/eval_jaxpr/ppermute | solution.py:11
  376.0 21.0 %collective-permute-start = (bf16[2,1024,2,128]{3,1,0,2:T(8,128)(2,1)}, bf16[2,1024,2,128]{3,1,0,2:T(8,128)(2,1)S(1)}, u32[]{:S(2)}, u32[]{:S(2)}) collective-permute-start(bf16[2,1024,2,128]{3,1,0,2:T(8,128)(2,1)} %get-tuple-element.195), channel_id=1, source_target_pairs={{0,16},{16,32},{32,48},{48,64},{64,80},{80,96},{96,112},{112,128},... | collective-permute-start | bytes 3145736 | tf_op jit(solution)/shard_map/while/body/eval_jaxpr/ppermute | solution.py:11
  399.3 21.0 %collective-permute-start = (bf16[2,1024,2,128]{3,1,0,2:T(8,128)(2,1)}, bf16[2,1024,2,128]{3,1,0,2:T(8,128)(2,1)S(1)}, u32[]{:S(2)}, u32[]{:S(2)}) collective-permute-start(bf16[2,1024,2,128]{3,1,0,2:T(8,128)(2,1)} %get-tuple-element.195), channel_id=1, source_target_pairs={{0,16},{16,32},{32,48},{48,64},{64,80},{80,96},{96,112},{112,128},... | collective-permute-start | bytes 3145736 | tf_op jit(solution)/shard_map/while/body/eval_jaxpr/ppermute | solution.py:11
  422.6 18.3 %collective-permute-start = (bf16[2,1024,2,128]{3,1,0,2:T(8,128)(2,1)}, bf16[2,1024,2,128]{3,1,0,2:T(8,128)(2,1)S(1)}, u32[]{:S(2)}, u32[]{:S(2)}) collective-permute-start(bf16[2,1024,2,128]{3,1,0,2:T(8,128)(2,1)} %get-tuple-element.195), channel_id=1, source_target_pairs={{0,16},{16,32},{32,48},{48,64},{64,80},{80,96},{96,112},{112,128},... | collective-permute-start | bytes 3145736 | tf_op jit(solution)/shard_map/while/body/eval_jaxpr/ppermute | solution.py:11
where the time goes:
time: 444 us; the launch traced here: 443 us
  waiting for transfers between devices  387 us (87%)
  matrix products  21.7 us (5%)
  local copies, waits for them, and re-layouts  21.4 us (5%)
  starting transfers between devices  8.36 us (2%)
  other arithmetic  4.68 us (1%)
    ppermute x15, waiting for transfers between devices, from_behind(): lax.ppermute(shard, axis, [(i, (i + by) % devices) for i in range(devices)])  360 us
    all_to_all x1, waiting for transfers between devices, body(): lax.all_to_all(whitened, 'win', split_axis=2, concat_axis=1, tiled=True)  26.6 us
    dot_general x16, matrix products, cross_block(): jnp.einsum('kpwfc,pwfd->fkcd', paired, held_block, preferred_element_type...  21.7 us
    while x15, local copies, waits for them, and re-layouts  14.5 us
  transfers between devices with their start and end apart: 16, of which 16 were waited for; matrix products, arithmetic and copies ran while one was open for 0% of the time, Pallas kernels for 0%

commit v1 on v0

v1 whole, which is shorter than its diff:
```python
import functools

import jax
import jax.numpy as jnp
from jax import lax
from jax.experimental import pallas as pl
from jax.experimental.pallas import tpu as pltpu
from jax.sharding import PartitionSpec as P

MESH = pl.DeviceIdType.MESH
F32, BF16 = jnp.float32, jnp.bfloat16

WIN = 16
SIDE = 4
BINS = 2
CH = 128
LW = 64
HALF = LW // 2
DEEP = WIN * HALF
FREQ = WIN * BINS


def mod4(v):
    return lax.rem(v + 2 * SIDE, SIDE)


def kernel(
    spec, mask, out,
    spec_v, send_v, g, t_own, t_row, acc, cross, res_send, res_recv, stage,
    in_sem, a_send, a_recv, g_send, g_recv, r_send, r_recv, s_send, s_recv, o_sem,
):
    chan, win = lax.axis_index("chan"), lax.axis_index("win")
    x, y = lax.rem(chan, SIDE), lax.div(chan, SIDE)

    def at(dx, dy):
        return mod4(y + dy) * SIDE + mod4(x + dx)

    barrier = pltpu.get_barrier_semaphore()

    def greet(k, _):
        pl.semaphore_signal(
            barrier, inc=1, device_id=(chan, lax.rem(win + k, WIN)), device_id_type=MESH
        )
        return 0

    lax.fori_loop(1, WIN, greet, 0)
    for d in (1, 2, 3):
        pl.semaphore_signal(barrier, inc=1, device_id=(at(d, 0), win), device_id_type=MESH)
        pl.semaphore_signal(barrier, inc=1, device_id=(at(0, d), win), device_id_type=MESH)

    rows = HALF * FREQ
    loads = [
        pltpu.make_async_copy(
            spec.at[:, pl.ds(h * rows, rows), :], spec_v.at[:, pl.ds(h * rows, rows), :], in_sem.at[h]
        )
        for h in range(2)
    ]
    for load in loads:
        load.start()

    def whiten(h):
        base = h * rows

        def add(f, total):
            for p in range(2):
                v = spec_v[p, pl.ds(base + f, HALF, stride=FREQ), :]
                total = total + v * v
            return total

        total = lax.fori_loop(0, FREQ, add, jnp.zeros((HALF, CH), F32))
        rms = jnp.sqrt(total * (1.0 / (2 * FREQ)) + 1e-6)
        factor = mask[pl.ds(h * HALF, HALF), :].astype(F32) / rms

        def scale(dst, _):
            for b in range(BINS):
                for p in range(2):
                    v = spec_v[p, pl.ds(base + dst * BINS + b, HALF, stride=FREQ), :]
                    send_v[h, b, dst, p] = (v * factor).astype(BF16)
            return 0

        lax.fori_loop(0, WIN, scale, 0)

    mine = pl.ds(pl.multiple_of(win * HALF, HALF), HALF)

    def spread(b, h):
        def one(k, _):
            dst = lax.rem(win + k, WIN)
            pltpu.make_async_remote_copy(
                src_ref=send_v.at[h, b, dst],
                dst_ref=g.at[0, b, h, :, mine, :],
                send_sem=a_send.at[b, h],
                recv_sem=a_recv.at[b, h],
                device_id=(chan, dst),
                device_id_type=MESH,
            ).start()
            return 0

        lax.fori_loop(1, WIN, one, 0)
        g[0, b, h, :, mine, :] = send_v[h, b, win]

    def spread_all(b, h):
        others = g.at[0, b, h, :, pl.ds(0, DEEP - HALF), :]
        return pltpu.make_async_remote_copy(
            src_ref=others, dst_ref=others, send_sem=a_send.at[b, h], recv_sem=a_recv.at[b, h],
            device_id=(chan, win), device_id_type=MESH,
        )

    sides = ((1, 0, 3), (-1, 0, 1), (0, 1, 6), (0, -1, 4))

    def direct(b, h):
        return [
            pltpu.make_async_remote_copy(
                src_ref=g.at[0, b, h], dst_ref=g.at[slot, b, h],
                send_sem=g_send.at[slot, b, h], recv_sem=g_recv.at[slot, b, h],
                device_id=(at(dx, dy), win), device_id_type=MESH,
            )
            for dx, dy, slot in sides
        ]

    def relay(b, h):
        return [
            pltpu.make_async_remote_copy(
                src_ref=g.at[slot, b, h, p], dst_ref=g.at[2 + 3 * (slot // 4), b, h, p],
                send_sem=r_send.at[slot, b, h], recv_sem=r_recv.at[slot, b, h],
                device_id=(at(dx, dy), win), device_id_type=MESH,
            )
            for (dx, dy, slot), p in zip(sides, (0, 1, 0, 1))
        ]

    def turned(slot, b, h, dst):
        a0, a1 = g[slot, b, h, 0].T, g[slot, b, h, 1].T
        dst[pl.ds(0, CH), pl.ds(0, DEEP)] = a0
        dst[pl.ds(0, CH), pl.ds(DEEP, DEEP)] = a1
        dst[pl.ds(CH, CH), pl.ds(0, DEEP)] = a1
        dst[pl.ds(CH, CH), pl.ds(DEEP, DEEP)] = -a0

    def product(lhs, slot, b, h):
        return jnp.dot(
            lhs[...], g[slot, b, h].reshape(2 * DEEP, CH), preferred_element_type=F32
        )

    scaling = 1.0 / 32.0

    def own(slot, b, h):
        part = product(t_own.at[b, h], slot, b, h)
        if h == 0:
            acc[slot, b] = part
        else:
            acc[slot, b] = (acc[slot, b] + part) * scaling

    def emit(value_ref, b, dx, dy):
        col = pl.multiple_of(at(dx, dy) * CH, CH)
        for k in range(2):
            pltpu.make_async_copy(
                value_ref.at[pl.ds(k * CH, CH), :], out.at[b, k, :, pl.ds(col, CH)], o_sem
            ).start()

    def give(value, dx, dy, b):
        n = (dx - 1) * 3 + (dy - 1)
        at_row = (3 - dx) * 3 + (dy - 1)
        at_col = (dx - 1) * 3 + (3 - dy)
        res_send[n, 0] = value.astype(BF16)
        res_send[n, 1, pl.ds(0, CH), :] = value[:CH].T.astype(BF16)
        res_send[n, 1, pl.ds(CH, CH), :] = (-value[CH:]).T.astype(BF16)
        for side, slot, dev in ((0, at_row, at(dx, 0)), (1, at_col, at(0, dy))):
            pltpu.make_async_remote_copy(
                src_ref=res_send.at[n, side], dst_ref=res_recv.at[slot, b],
                send_sem=s_send.at[n, side], recv_sem=s_recv.at[slot, b],
                device_id=(dev, win), device_id_type=MESH,
            ).start()

    def pair(lhs, dx, dy, b, h, keep):
        part = product(lhs, 3 + dy, b, h)
        if h == 0:
            cross[keep] = part
        else:
            give((cross[keep] + part) * scaling, dx, dy, b)

    def early(b, h):
        def one(i, _):
            own(i + lax.div(i, 2), b, h)
            return 0

        lax.fori_loop(0, 5, one, 0)

    def late(b, h):
        for slot in (2, 5):
            own(slot, b, h)
        near = 1 if b == 0 else 3
        turned(near, b, h, t_row.at[2, h])
        turned(2, b, h, t_row.at[b, h])

        def one(i, _):
            pair(t_row.at[2, h], near, i + 1, b, h, i)
            return 0

        lax.fori_loop(0, 3, one, 0)
        pair(t_row.at[b, h], 2, near, b, h, 3)
        if h == 1:
            for slot in range(7):
                emit(acc.at[slot, b], b, slot if slot < 4 else 0, slot - 3 if slot > 3 else 0)

    units = [(b, h) for b in range(BINS) for h in range(2)]

    loads[0].wait()
    whiten(0)
    pl.semaphore_wait(barrier, WIN - 1 + 2 * (SIDE - 1))
    spread(0, 0)
    loads[1].wait()
    whiten(1)
    spread(0, 1)
    for step in range(len(units) + 2):
        if step < len(units):
            unit = units[step]
            spread_all(*unit).wait_recv()
            for copy in direct(*unit):
                copy.start()
            if step + 2 < len(units):
                spread(*units[step + 2])
            turned(0, *unit, t_own.at[unit])
        if 0 <= step - 1 < len(units):
            unit = units[step - 1]
            for copy, onward in zip(direct(*unit), relay(*unit)):
                copy.wait_recv()
                onward.start()
            early(*unit)
        if 0 <= step - 2 < len(units):
            unit = units[step - 2]
            for copy in relay(*unit):
                copy.wait_recv()
            late(*unit)

    bin_here = lax.div(x, 2)
    value = product(t_row.at[bin_here, 0], 5, bin_here, 0)
    value = value + product(t_row.at[bin_here, 1], 5, bin_here, 1)
    give(value * scaling, 2, 2, bin_here)

    def arrived(slot, b):
        return pltpu.make_async_remote_copy(
            src_ref=res_recv.at[slot, b], dst_ref=res_recv.at[slot, b],
            send_sem=s_send.at[slot, 0], recv_sem=s_recv.at[slot, b],
            device_id=(chan, win), device_id_type=MESH,
        )

    for b in range(BINS):
        def take(n, _):
            arrived(n, b).wait_recv()
            stage[n, b] = res_recv[n, b].astype(F32)
            emit(stage.at[n, b], b, lax.div(n, 3) + 1, lax.rem(n, 3) + 1)
            return 0

        lax.fori_loop(0, 9, take, 0)

    for unit in units:
        spread_all(*unit).wait_send()
        for copy in direct(*unit) + relay(*unit):
            copy.wait_send()

    def gone(n, _):
        for side in range(2):
            pltpu.make_async_remote_copy(
                src_ref=res_send.at[n, side], dst_ref=res_send.at[n, side],
                send_sem=s_send.at[n, side], recv_sem=s_recv.at[n, 0],
                device_id=(chan, win), device_id_type=MESH,
            ).wait_send()
        return 0

    lax.fori_loop(0, 9, gone, 0)
    pltpu.make_async_copy(out, out, o_sem).wait()


def body(spectra, quality_mask):
    flat = spectra.reshape(2, LW * FREQ, CH)
    dma = pltpu.SemaphoreType.DMA
    return pl.pallas_call(
        kernel,
        out_shape=jax.ShapeDtypeStruct((BINS, 2, CH, CH * SIDE * SIDE), F32),
        in_specs=[pl.BlockSpec(memory_space=pl.ANY), pl.BlockSpec(memory_space=pltpu.VMEM)],
        out_specs=pl.BlockSpec(memory_space=pl.ANY),
        scratch_shapes=[
            pltpu.VMEM((2, LW * FREQ, CH), F32),
            pltpu.VMEM((2, BINS, WIN, 2, HALF, CH), BF16),
            pltpu.VMEM((7, BINS, 2, 2, DEEP, CH), BF16),
            pltpu.VMEM((BINS, 2, 2 * CH, 2 * DEEP), BF16),
            pltpu.VMEM((3, 2, 2 * CH, 2 * DEEP), BF16),
            pltpu.VMEM((7, BINS, 2 * CH, CH), F32),
            pltpu.VMEM((4, 2 * CH, CH), F32),
            pltpu.VMEM((9, 2, 2 * CH, CH), BF16),
            pltpu.VMEM((9, BINS, 2 * CH, CH), BF16),
            pltpu.VMEM((9, BINS, 2 * CH, CH), F32),
            dma((2,)),
            dma((BINS, 2)),
            dma((BINS, 2)),
            dma((7, BINS, 2)),
            dma((7, BINS, 2)),
            dma((7, BINS, 2)),
            dma((7, BINS, 2)),
            dma((9, 2)),
            dma((9, BINS)),
            dma(()),
        ],
        compiler_params=pltpu.CompilerParams(
            collective_id=0, has_side_effects=True, vmem_limit_bytes=48 * 1024 * 1024
        ),
        cost_estimate=pl.CostEstimate(
            flops=6_200_000_000, bytes_accessed=6 * 1024 * 1024, transcendentals=0
        ),
    )(flat, quality_mask)


def solution(mesh):
    placed = (P(None, "win", None, "chan"), P("win", "chan"))
    return jax.shard_map(
        body, mesh=mesh, in_specs=placed, out_specs=P("win", None, "chan", None), check_vma=False
    )
```

time: 444 us -> 78.7 us (0.18)
  the two profiles are of different devices: /device:TPU:0 before, /device:TPU:1 now
where the time goes in v1:
time: 78.7 us; the launch traced here: 78.3 us
  Pallas kernels  71.2 us (90%)
  local copies, waits for them, and re-layouts  7.05 us (9%)
    pallas_call x1, Pallas kernels, body(): pl.pallas_call(kernel, out_shape=jax.ShapeDtypeStruct((BINS, 2, CH, CH *...  71.2 us
    unnamed x5, local copies, waits for them, and re-layouts  7.05 us

profile of v1, /device:TPU:1, one launch (start us, length us, event | category | flops | bytes accessed | tf_op | source)
XLA Modules:
  0.0 78.3 jit_solution(157590209828489076)
XLA Ops:
  0.0 0.0 copy-start
  0.0 1.6 %copy-done = f32[2,64,32,128]{3,2,1,0:T(8,128)S(1)} copy-done((f32[2,64,32,128]{3,2,1,0:T(8,128)S(1)}, f32[2,64,32,128]{3,2,1,0:T(8,128)}, u32[]{:S(2)}) %copy-start) | copy-done | bytes 2097176
  1.6 0.0 copy-start.1
  1.6 0.8 copy-done.1
  2.4 71.2 %shard_map.28 = f32[2,2,128,2048]{3,2,1,0:T(8,128)} custom-call(f32[2,2048,128]{2,1,0:T(8,128)S(1)} %bitcast.1, s32[64,128]{1,0:T(8,128)S(1)} %copy-done.1), custom_call_target="tpu_custom_call" | custom-call | flops 6200000000 | bytes 6291456 | tf_op jit(solution)/shard_map/pallas_call | solution.py:275
  73.6 4.7 %copy.4 = f32[2,2,128,2048]{3,2,1,0:T(8,128)} copy(f32[2,2,128,2048]{3,2,1,0:T(8,128)} %shard_map.28) | data formatting | bytes 8388608
Async XLA Ops:
  0.0 1.6 %copy-start = (f32[2,64,32,128]{3,2,1,0:T(8,128)S(1)}, f32[2,64,32,128]{3,2,1,0:T(8,128)}, u32[]{:S(2)}) copy-start(f32[2,64,32,128]{3,2,1,0:T(8,128)} %param.2) | copy-start | bytes 6291460
  1.6 0.8 copy-start.1

commit v2 on v0

v2 whole, which is shorter than its diff:
```python
import jax
import jax.numpy as jnp
from jax import lax
from jax.experimental import pallas as pl
from jax.experimental.pallas import tpu as pltpu
from jax.sharding import PartitionSpec as P

MESH = pl.DeviceIdType.MESH
F32, BF16 = jnp.float32, jnp.bfloat16

WIN = 16
SIDE = 4
BINS = 2
FREQ = WIN * BINS
CH = 128
LW = 64
PARTS = 2
PW = LW // PARTS
AHEAD = 2
UNITS = BINS * PARTS
DEEP = WIN * PW
ROWS = PW * FREQ
SCALE = 1.0 / 32.0

PLACES = ((0, 0), (1, 0), (2, 0), (1, 1), (0, 1), (0, 2))
FOREIGN = ((-1, 0), (0, -1), (-1, -1), (-1, 1), (1, -1), (-2, 1), (2, -1), (1, -2), (-1, 2), (2, 2))
MATES = ((1, 0), (-1, 0), (2, 0), (0, 1), (0, -1), (0, 2), (1, 1), (-1, -1))


def kernel(
    spec, mask_hbm, out,
    spec_v, mask, send_v, g, turned, acc, res_send, res_recv,
    in_sem, a_send, a_recv, d_send, d_recv, r_send, r_recv, s_send, s_recv,
):
    chan, win = lax.axis_index("chan"), lax.axis_index("win")
    x, y = lax.rem(chan, SIDE), lax.div(chan, SIDE)
    way = 1 - 2 * lax.rem(win, 2)

    def at(place):
        dx, dy = place
        return lax.rem(y + way * dy + 2 * SIDE, SIDE) * SIDE + lax.rem(x + way * dx + 2 * SIDE, SIDE)

    barrier = pltpu.get_barrier_semaphore()

    def greet(k, _):
        pl.semaphore_signal(
            barrier, inc=1, device_id=(chan, lax.rem(win + k, WIN)), device_id_type=MESH
        )
        return 0

    lax.fori_loop(1, WIN, greet, 0)
    for place in MATES:
        pl.semaphore_signal(barrier, inc=1, device_id=(at(place), win), device_id_type=MESH)

    loads = [pltpu.make_async_copy(mask_hbm, mask, in_sem.at[PARTS])]
    for q in range(PARTS):
        rows = pl.ds(q * ROWS, ROWS)
        loads.append(pltpu.make_async_copy(spec.at[:, rows, :], spec_v.at[:, rows, :], in_sem.at[q]))
    for load in loads:
        load.start()

    def whiten(q):
        def add(f, total):
            for p in range(2):
                v = spec_v[p, pl.ds(q * ROWS + f, PW, stride=FREQ), :]
                total = total + v * v
            return total

        total = lax.fori_loop(0, FREQ, add, jnp.zeros((PW, CH), F32))
        rms = jnp.sqrt(total * (1.0 / (2 * FREQ)) + 1e-6)
        factor = mask[pl.ds(q * PW, PW), :].astype(F32) / rms

        def scale(dst, _):
            for b in range(BINS):
                for p in range(2):
                    v = spec_v[p, pl.ds(q * ROWS + dst * BINS + b, PW, stride=FREQ), :]
                    send_v[b * PARTS + q, dst, p] = (v * factor).astype(BF16)
            return 0

        lax.fori_loop(0, WIN, scale, 0)

    mine = pl.ds(pl.multiple_of(win * PW, PW), PW)

    def spread(u):
        def one(k, _):
            dst = lax.rem(win + k, WIN)
            pltpu.make_async_remote_copy(
                src_ref=send_v.at[u, dst], dst_ref=g.at[0, u, :, mine, :],
                send_sem=a_send.at[u], recv_sem=a_recv.at[u],
                device_id=(chan, dst), device_id_type=MESH,
            ).start()
            return 0

        lax.fori_loop(1, WIN, one, 0)
        g[0, u, :, mine, :] = send_v[u, win]

    def spread_all(u):
        others = g.at[0, u, :, pl.ds(0, DEEP - PW), :]
        return pltpu.make_async_remote_copy(
            src_ref=others, dst_ref=others, send_sem=a_send.at[u], recv_sem=a_recv.at[u],
            device_id=(chan, win), device_id_type=MESH,
        )

    def remote(src, dst, send, recv, place):
        return pltpu.make_async_remote_copy(
            src_ref=src, dst_ref=dst, send_sem=send, recv_sem=recv,
            device_id=(at(place), win), device_id_type=MESH,
        )

    def direct(u):
        return [
            remote(g.at[0, u], g.at[slot, u], d_send.at[u, i], d_recv.at[u, i], place)
            for i, (slot, place) in enumerate(((1, (-1, 0)), (4, (0, -1))))
        ]

    def relay(u):
        moves = (
            (g.at[1, u], g.at[2, u], (-1, 0)),
            (g.at[1, u, 0], g.at[3, u, 0], (0, -1)),
            (g.at[4, u], g.at[5, u], (0, -1)),
            (g.at[4, u, 1], g.at[3, u, 1], (-1, 0)),
        )
        return [
            remote(src, dst, r_send.at[u, i], r_recv.at[u, i], place)
            for i, (src, dst, place) in enumerate(moves)
        ]

    def turn(slot, u):
        a0, a1 = g[slot, u, 0].T, g[slot, u, 1].T
        turned[slot, pl.ds(0, CH), pl.ds(0, DEEP)] = a0
        turned[slot, pl.ds(0, CH), pl.ds(DEEP, DEEP)] = a1
        turned[slot, pl.ds(CH, CH), pl.ds(0, DEEP)] = a1
        turned[slot, pl.ds(CH, CH), pl.ds(DEEP, DEEP)] = -a0

    def add_product(group, u, lhs, right):
        rhs = jnp.concatenate([g[s, u].reshape(2 * DEEP, CH) for s in right], axis=1)
        part = jnp.dot(turned[lhs], rhs, preferred_element_type=F32)
        acc[group, :, pl.ds(0, CH * len(right))] += part

    def result(group, i):
        return acc[group, :, pl.ds(i * CH, CH)] * SCALE

    def column(place):
        return pl.ds(pl.multiple_of(at(place) * CH, CH), CH)

    def keep(b, place, value):
        for k in range(2):
            out[b, k, :, column(place)] = value[k * CH : (k + 1) * CH]

    def send(b, m, slot, place):
        remote(
            res_send.at[b, m], res_recv.at[b, slot], s_send.at[b, m], s_recv.at[b, slot], place
        ).start()

    def give(b, m, slot, place, value):
        res_send[b, m] = value.astype(BF16)
        pl.when(b == BINS - 1)(lambda: send(b, m, slot, place))

    def give_turned(b, m, slot, place, value):
        res_send[b, m, pl.ds(0, CH), :] = value[:CH].T.astype(BF16)
        res_send[b, m, pl.ds(CH, CH), :] = (-value[CH:]).T.astype(BF16)
        pl.when(b == BINS - 1)(lambda: send(b, m, slot, place))

    half = lax.div(x, 2)

    def compute(u):
        b, q = lax.div(u, PARTS), lax.rem(u, PARTS)
        last = q == PARTS - 1
        for slot in range(3):
            turn(slot, u)

        @pl.when(b == half)
        def _():
            add_product(4, u, 2, (4, 5))

        @pl.when(b != half)
        def _():
            add_product(4, u, 2, (4,))

        @pl.when(last)
        def _():
            @pl.when(b == half)
            def _():
                v = result(4, 1)
                give(b, 9, 9, (2, 0), v)
                give_turned(b, 10, 9, (0, 2), v)

            v = result(4, 0)
            give(b, 5, 5, (2, 0), v)
            give_turned(b, 6, 6, (0, 1), v)

        add_product(3, u, 1, (4, 5))

        @pl.when(last)
        def _():
            v = result(3, 1)
            give_turned(b, 7, 7, (0, 2), v)
            give(b, 8, 8, (1, 0), v)
            v = result(3, 0)
            give(b, 3, 3, (1, 0), v)
            give_turned(b, 4, 4, (0, 1), v)

        add_product(1, u, 0, (2, 3))

        @pl.when(last)
        def _():
            v = result(1, 1)
            give_turned(b, 2, 2, (1, 1), v)
            keep(b, (1, 1), v)
            keep(b, (2, 0), result(1, 0))

        add_product(0, u, 0, (0, 1))

        @pl.when(last)
        def _():
            v = result(0, 1)
            give_turned(b, 0, 0, (1, 0), v)
            keep(b, (1, 0), v)
            keep(b, (0, 0), result(0, 0))

        add_product(2, u, 0, (4, 5))

        @pl.when(last)
        def _():
            v = result(2, 0)
            give_turned(b, 1, 1, (0, 1), v)
            keep(b, (0, 1), v)
            keep(b, (0, 2), result(2, 1))
            acc[...] = jnp.zeros_like(acc)

    def send_first():
        for m, place in enumerate(
            ((1, 0), (0, 1), (1, 1), (1, 0), (0, 1), (2, 0), (0, 1), (0, 2), (1, 0))
        ):
            send(0, m, m, place)

        @pl.when(half == 0)
        def _():
            send(0, 9, 9, (2, 0))
            send(0, 10, 9, (0, 2))

    def take(b):
        for slot, place in enumerate(FOREIGN):
            remote(
                res_recv.at[b, slot], res_recv.at[b, slot], s_send.at[b, slot], s_recv.at[b, slot], (0, 0)
            ).wait_recv()
            keep(b, place, res_recv[b, slot].astype(F32))

    acc[...] = jnp.zeros_like(acc)
    loads[0].wait()
    loads[1].wait()
    whiten(0)
    pl.semaphore_wait(barrier, WIN - 1 + len(MATES))
    spread(0)
    for q in range(1, PARTS):
        loads[1 + q].wait()
        whiten(q)
    for u in range(1, AHEAD):
        spread(u)

    def step(t, _):
        @pl.when(t < UNITS)
        def _():
            spread_all(t).wait_recv()
            for copy in direct(t):
                copy.start()

        @pl.when(t + AHEAD < UNITS)
        def _():
            spread(t + AHEAD)

        @pl.when((t >= 1) & (t <= UNITS))
        def _():
            here, onward = direct(t - 1), relay(t - 1)
            here[0].wait_recv()
            onward[0].start()
            onward[1].start()
            here[1].wait_recv()
            onward[2].start()
            onward[3].start()

        @pl.when(t >= 2)
        def _():
            for copy in relay(t - 2):
                copy.wait_send()
            pl.when(t == UNITS + 1)(send_first)
            for copy in relay(t - 2):
                copy.wait_recv()
            compute(t - 2)

        return 0

    lax.fori_loop(0, UNITS + 2, step, 0)
    take(0)
    take(1)

    def sent(u, _):
        spread_all(u).wait_send()
        for copy in direct(u):
            copy.wait_send()
        return 0

    lax.fori_loop(0, UNITS, sent, 0)

    def gone(b, m):
        remote(
            res_send.at[b, m], res_send.at[b, m], s_send.at[b, m], s_recv.at[b, 0], (0, 0)
        ).wait_send()

    for b in range(BINS):
        for m in range(9):
            gone(b, m)
    gone(half, 9)
    gone(half, 10)


def body(spectra, quality_mask):
    flat = spectra.reshape(2, LW * FREQ, CH)
    dma = pltpu.SemaphoreType.DMA
    return pl.pallas_call(
        kernel,
        out_shape=pltpu.VMEM((BINS, 2, CH, CH * SIDE * SIDE), F32),
        in_specs=[pl.BlockSpec(memory_space=pltpu.HBM)] * 2,
        out_specs=pl.BlockSpec(memory_space=pltpu.VMEM),
        scratch_shapes=[
            pltpu.VMEM((2, LW * FREQ, CH), F32),
            pltpu.VMEM((LW, CH), jnp.int32),
            pltpu.VMEM((UNITS, WIN, 2, PW, CH), BF16),
            pltpu.VMEM((len(PLACES), UNITS, 2, DEEP, CH), BF16),
            pltpu.VMEM((3, 2 * CH, 2 * DEEP), BF16),
            pltpu.VMEM((5, 2 * CH, 2 * CH), F32),
            pltpu.VMEM((BINS, 11, 2 * CH, CH), BF16),
            pltpu.VMEM((BINS, 10, 2 * CH, CH), BF16),
            dma((PARTS + 1,)),
            dma((UNITS,)),
            dma((UNITS,)),
            dma((UNITS, 2)),
            dma((UNITS, 2)),
            dma((UNITS, 4)),
            dma((UNITS, 4)),
            dma((BINS, 11)),
            dma((BINS, 10)),
        ],
        compiler_params=pltpu.CompilerParams(
            collective_id=0, has_side_effects=True, vmem_limit_bytes=40 * 1024 * 1024
        ),
        cost_estimate=pl.CostEstimate(
            flops=5_200_000_000, bytes_accessed=6 * 1024 * 1024, transcendentals=0
        ),
    )(*(pltpu.with_memory_space_constraint(a, pltpu.HBM) for a in (flat, quality_mask)))


def solution(mesh):
    placed = (P(None, "win", None, "chan"), P("win", "chan"))
    return jax.shard_map(
        body, mesh=mesh, in_specs=placed, out_specs=P("win", None, "chan", None), check_vma=False
    )
```

time: 444 us -> 66 us (0.15)
  the two profiles are of different devices: /device:TPU:0 before, /device:TPU:1 now
where the time goes in v2:
time: 66 us; the launch traced here: 65.9 us
  Pallas kernels  63.8 us (97%)
  local copies, waits for them, and re-layouts  2.02 us (3%)
    pallas_call x1, Pallas kernels, body(): pl.pallas_call(kernel, out_shape=pltpu.VMEM((BINS, 2, CH, CH * SIDE * SID...  63.8 us
    unnamed x1, local copies, waits for them, and re-layouts  2.02 us

profile of v2, /device:TPU:1, one launch (start us, length us, event | category | flops | bytes accessed | tf_op | source)
XLA Modules:
  0.0 65.9 jit_solution(5812395351977607538)
XLA Ops:
  0.0 63.8 %shard_map.28 = f32[2,2,128,2048]{3,2,1,0:T(8,128)S(1)} custom-call(f32[2,2048,128]{2,1,0:T(8,128)} %bitcast.1, s32[64,128]{1,0:T(8,128)} %mask_hbm.1), custom_call_target="tpu_custom_call" | custom-call | flops 5200000000 | bytes 6291456 | tf_op jit(solution)/shard_map/pallas_call | solution.py:320
  63.9 2.0 %copy.4 = f32[2,2,128,2048]{3,2,1,0:T(8,128)} copy(f32[2,2,128,2048]{3,2,1,0:T(8,128)S(1)} %shard_map.28) | data formatting | bytes 8388608

commit v3 on v2

--- a/solution.py
+++ b/solution.py
@@ -14,9 +14,11 @@
 FREQ = WIN * BINS
 CH = 128
 LW = 64
-PARTS = 2
+PARTS = 4
 PW = LW // PARTS
 AHEAD = 2
+EARLY, LATE = 1, 4
+SEND_NEAR, SEND_FAR = 9, 9
 UNITS = BINS * PARTS
 DEEP = WIN * PW
 ROWS = PW * FREQ
@@ -29,7 +31,7 @@
 
 def kernel(
     spec, mask_hbm, out,
-    spec_v, mask, send_v, g, turned, acc, res_send, res_recv,
+    spec_v, mask, send_v, g, turned, turned_far, acc, res_send, res_recv,
     in_sem, a_send, a_recv, d_send, d_recv, r_send, r_recv, s_send, s_recv,
 ):
     chan, win = lax.axis_index("chan"), lax.axis_index("win")
@@ -125,17 +127,19 @@
             for i, (src, dst, place) in enumerate(moves)
         ]
 
-    def turn(slot, u):
+    def turn(slot, u, dst):
         a0, a1 = g[slot, u, 0].T, g[slot, u, 1].T
-        turned[slot, pl.ds(0, CH), pl.ds(0, DEEP)] = a0
-        turned[slot, pl.ds(0, CH), pl.ds(DEEP, DEEP)] = a1
-        turned[slot, pl.ds(CH, CH), pl.ds(0, DEEP)] = a1
-        turned[slot, pl.ds(CH, CH), pl.ds(DEEP, DEEP)] = -a0
-
-    def add_product(group, u, lhs, right):
-        rhs = jnp.concatenate([g[s, u].reshape(2 * DEEP, CH) for s in right], axis=1)
-        part = jnp.dot(turned[lhs], rhs, preferred_element_type=F32)
-        acc[group, :, pl.ds(0, CH * len(right))] += part
+        dst[pl.ds(0, CH), pl.ds(0, DEEP)] = a0
+        dst[pl.ds(0, CH), pl.ds(DEEP, DEEP)] = a1
+        dst[pl.ds(CH, CH), pl.ds(0, DEEP)] = a1
+        dst[pl.ds(CH, CH), pl.ds(DEEP, DEEP)] = -a0
+
+    def add_product(group, at_col, u, lhs, right):
+        rhs = [g[s, u].reshape(2 * DEEP, CH) for s in right]
+        rhs = rhs[0] if len(rhs) == 1 else jnp.concatenate(rhs, axis=1)
+        left = turned_far[...] if lhs == 2 else turned[u, lhs]
+        part = jnp.dot(left, rhs, preferred_element_type=F32)
+        acc[group, :, pl.ds(at_col * CH, CH * len(right))] += part
 
     def result(group, i):
         return acc[group, :, pl.ds(i * CH, CH)] * SCALE
@@ -152,92 +156,114 @@
             res_send.at[b, m], res_recv.at[b, slot], s_send.at[b, m], s_recv.at[b, slot], place
         ).start()
 
-    def give(b, m, slot, place, value):
+    def give(b, m, value):
         res_send[b, m] = value.astype(BF16)
-        pl.when(b == BINS - 1)(lambda: send(b, m, slot, place))
-
-    def give_turned(b, m, slot, place, value):
+
+    def give_turned(b, m, value):
         res_send[b, m, pl.ds(0, CH), :] = value[:CH].T.astype(BF16)
         res_send[b, m, pl.ds(CH, CH), :] = (-value[CH:]).T.astype(BF16)
-        pl.when(b == BINS - 1)(lambda: send(b, m, slot, place))
 
     half = lax.div(x, 2)
 
-    def compute(u):
+    def early(u):
         b, q = lax.div(u, PARTS), lax.rem(u, PARTS)
-        last = q == PARTS - 1
-        for slot in range(3):
-            turn(slot, u)
+        turn(0, u, turned.at[u, 0])
+        turn(1, u, turned.at[u, 1])
+        add_product(2, 0, u, 1, (4,))
+        add_product(0, 0, u, 0, (0, 1))
+        add_product(1, 0, u, 0, (4,))
+
+        @pl.when(q == PARTS - 1)
+        def _():
+            v = result(2, 0)
+            give(b, 3, v)
+            give_turned(b, 4, v)
+            v = result(0, 1)
+            give_turned(b, 0, v)
+            keep(b, (1, 0), v)
+            v = result(1, 0)
+            give_turned(b, 1, v)
+            keep(b, (0, 1), v)
+            keep(b, (0, 0), result(0, 0))
+            acc[0] = jnp.zeros_like(acc[0])
+            for group in (1, 2):
+                acc[group, :, pl.ds(0, CH)] = jnp.zeros((2 * CH, CH), F32)
+
+    def send_early(b):
+        for m, place in ((3, (1, 0)), (4, (0, 1)), (0, (1, 0)), (1, (0, 1))):
+            send(b, m, m, place)
+
+    def send_far(b):
+        send(b, 5, 5, (2, 0))
+        send(b, 6, 6, (0, 1))
+
+    def send_both(b):
+        send(b, 9, 9, (2, 0))
+        send(b, 10, 9, (0, 2))
+
+    def send_side(b):
+        send(b, 7, 7, (0, 2))
+        send(b, 8, 8, (1, 0))
+
+    def send_diagonal(b):
+        send(b, 2, 2, (1, 1))
+
+    def late(u):
+        b, q = lax.div(u, PARTS), lax.rem(u, PARTS)
+        done = q == PARTS - 1
+        now = done & (b == BINS - 1)
+        turn(2, u, turned_far)
 
         @pl.when(b == half)
         def _():
-            add_product(4, u, 2, (4, 5))
+            add_product(4, 0, u, 2, (4, 5))
 
         @pl.when(b != half)
         def _():
-            add_product(4, u, 2, (4,))
-
-        @pl.when(last)
+            add_product(4, 0, u, 2, (4,))
+
+        @pl.when(done)
         def _():
             @pl.when(b == half)
             def _():
                 v = result(4, 1)
-                give(b, 9, 9, (2, 0), v)
-                give_turned(b, 10, 9, (0, 2), v)
+                give(b, 9, v)
+                give_turned(b, 10, v)
+                pl.when(now)(lambda: send_both(b))
 
             v = result(4, 0)
-            give(b, 5, 5, (2, 0), v)
-            give_turned(b, 6, 6, (0, 1), v)
-
-        add_product(3, u, 1, (4, 5))
-
-        @pl.when(last)
+            give(b, 5, v)
+            give_turned(b, 6, v)
+            pl.when(now)(lambda: send_far(b))
+
+        add_product(2, 1, u, 1, (5,))
+
+        @pl.when(done)
+        def _():
+            v = result(2, 1)
+            give_turned(b, 7, v)
+            give(b, 8, v)
+            pl.when(now)(lambda: send_side(b))
+
+        add_product(3, 0, u, 0, (2, 3))
+
+        @pl.when(done)
         def _():
             v = result(3, 1)
-            give_turned(b, 7, 7, (0, 2), v)
-            give(b, 8, 8, (1, 0), v)
-            v = result(3, 0)
-            give(b, 3, 3, (1, 0), v)
-            give_turned(b, 4, 4, (0, 1), v)
-
-        add_product(1, u, 0, (2, 3))
-
-        @pl.when(last)
-        def _():
-            v = result(1, 1)
-            give_turned(b, 2, 2, (1, 1), v)
+            give_turned(b, 2, v)
+            pl.when(now)(lambda: send_diagonal(b))
             keep(b, (1, 1), v)
-            keep(b, (2, 0), result(1, 0))
-
-        add_product(0, u, 0, (0, 1))
-
-        @pl.when(last)
-        def _():
-            v = result(0, 1)
-            give_turned(b, 0, 0, (1, 0), v)
-            keep(b, (1, 0), v)
-            keep(b, (0, 0), result(0, 0))
-
-        add_product(2, u, 0, (4, 5))
-
-        @pl.when(last)
-        def _():
-            v = result(2, 0)
-            give_turned(b, 1, 1, (0, 1), v)
-            keep(b, (0, 1), v)
-            keep(b, (0, 2), result(2, 1))
-            acc[...] = jnp.zeros_like(acc)
-
-    def send_first():
-        for m, place in enumerate(
-            ((1, 0), (0, 1), (1, 1), (1, 0), (0, 1), (2, 0), (0, 1), (0, 2), (1, 0))
-        ):
-            send(0, m, m, place)
-
-        @pl.when(half == 0)
-        def _():
-            send(0, 9, 9, (2, 0))
-            send(0, 10, 9, (0, 2))
+            keep(b, (2, 0), result(3, 0))
+
+        add_product(1, 1, u, 0, (5,))
+
+        @pl.when(done)
+        def _():
+            keep(b, (0, 2), result(1, 1))
+            for group in (1, 2):
+                acc[group, :, pl.ds(CH, CH)] = jnp.zeros((2 * CH, CH), F32)
+            for group in (3, 4):
+                acc[group] = jnp.zeros_like(acc[group])
 
     def take(b):
         for slot, place in enumerate(FOREIGN):
@@ -279,25 +305,46 @@
             onward[2].start()
             onward[3].start()
 
-        @pl.when(t >= 2)
-        def _():
-            for copy in relay(t - 2):
+        @pl.when((t >= EARLY) & (t < UNITS + EARLY))
+        def _():
+            early(t - EARLY)
+
+        pl.when(t == SEND_NEAR)(lambda: send_early(0))
+
+        @pl.when(t == UNITS + 1)
+        def _():
+            for copy in relay(UNITS - 1):
                 copy.wait_send()
-            pl.when(t == UNITS + 1)(send_first)
-            for copy in relay(t - 2):
+            send_early(1)
+
+        @pl.when(t == SEND_FAR)
+        def _():
+            send_far(0)
+            send_side(0)
+            send_diagonal(0)
+            pl.when(half == 0)(lambda: send_both(0))
+
+        @pl.when(t >= LATE)
+        def _():
+            for copy in relay(t - LATE):
                 copy.wait_recv()
-            compute(t - 2)
+            late(t - LATE)
 
         return 0
 
-    lax.fori_loop(0, UNITS + 2, step, 0)
+    lax.fori_loop(0, UNITS + LATE, step, 0)
     take(0)
-    take(1)
 
     def sent(u, _):
         spread_all(u).wait_send()
         for copy in direct(u):
             copy.wait_send()
+
+        @pl.when(u < UNITS - 1)
+        def _():
+            for copy in relay(u):
+                copy.wait_send()
+
         return 0
 
     lax.fori_loop(0, UNITS, sent, 0)
@@ -307,11 +354,13 @@
             res_send.at[b, m], res_send.at[b, m], s_send.at[b, m], s_recv.at[b, 0], (0, 0)
         ).wait_send()
 
-    for b in range(BINS):
-        for m in range(9):
-            gone(b, m)
-    gone(half, 9)
-    gone(half, 10)
+    for m in range(9):
+        gone(0, m)
+    pl.when(half == 0)(lambda: (gone(0, 9), gone(0, 10), None)[2])
+    take(1)
+    for m in range(9):
+        gone(1, m)
+    pl.when(half == 1)(lambda: (gone(1, 9), gone(1, 10), None)[2])
 
 
 def body(spectra, quality_mask):
@@ -327,7 +376,8 @@
             pltpu.VMEM((LW, CH), jnp.int32),
             pltpu.VMEM((UNITS, WIN, 2, PW, CH), BF16),
             pltpu.VMEM((len(PLACES), UNITS, 2, DEEP, CH), BF16),
-            pltpu.VMEM((3, 2 * CH, 2 * DEEP), BF16),
+            pltpu.VMEM((UNITS, 2, 2 * CH, 2 * DEEP), BF16),
+            pltpu.VMEM((2 * CH, 2 * DEEP), BF16),
             pltpu.VMEM((5, 2 * CH, 2 * CH), F32),
             pltpu.VMEM((BINS, 11, 2 * CH, CH), BF16),
             pltpu.VMEM((BINS, 10, 2 * CH, CH), BF16),

time: 66 us -> 64.1 us (0.971)
  Pallas kernels: 63.8 us -> 61.5 us
    pallas_call x1, Pallas kernels: 63.8 us -> 61.5 us  [body(): pl.pallas_call(kernel, out_shape=pltpu.VMEM((BINS, 2, CH, CH * SIDE * SID...]
where the time goes in v3:
time: 64.1 us; the launch traced here: 63.5 us
  Pallas kernels  61.5 us (96%)
  local copies, waits for them, and re-layouts  2.02 us (3%)
    pallas_call x1, Pallas kernels, body(): pl.pallas_call(kernel, out_shape=pltpu.VMEM((BINS, 2, CH, CH * SIDE * SID...  61.5 us
    unnamed x1, local copies, waits for them, and re-layouts  2.02 us

profile of v3, /device:TPU:1, one launch (start us, length us, event | category | flops | bytes accessed | tf_op | source)
XLA Modules:
  0.0 63.5 jit_solution(14449501960271981304)
XLA Ops:
  0.0 61.5 %shard_map.28 = f32[2,2,128,2048]{3,2,1,0:T(8,128)S(1)} custom-call(f32[2,2048,128]{2,1,0:T(8,128)} %bitcast.1, s32[64,128]{1,0:T(8,128)} %mask_hbm.1), custom_call_target="tpu_custom_call" | custom-call | flops 5200000000 | bytes 6291456 | tf_op jit(solution)/shard_map/pallas_call | solution.py:369
  61.5 2.0 %copy.4 = f32[2,2,128,2048]{3,2,1,0:T(8,128)} copy(f32[2,2,128,2048]{3,2,1,0:T(8,128)S(1)} %shard_map.28) | data formatting | bytes 8388608

commit v4 on v3

--- a/solution.py
+++ b/solution.py
@@ -42,18 +42,6 @@
         dx, dy = place
         return lax.rem(y + way * dy + 2 * SIDE, SIDE) * SIDE + lax.rem(x + way * dx + 2 * SIDE, SIDE)
 
-    barrier = pltpu.get_barrier_semaphore()
-
-    def greet(k, _):
-        pl.semaphore_signal(
-            barrier, inc=1, device_id=(chan, lax.rem(win + k, WIN)), device_id_type=MESH
-        )
-        return 0
-
-    lax.fori_loop(1, WIN, greet, 0)
-    for place in MATES:
-        pl.semaphore_signal(barrier, inc=1, device_id=(at(place), win), device_id_type=MESH)
-
     loads = [pltpu.make_async_copy(mask_hbm, mask, in_sem.at[PARTS])]
     for q in range(PARTS):
         rows = pl.ds(q * ROWS, ROWS)
@@ -61,6 +49,18 @@
     for load in loads:
         load.start()
 
+    barrier = pltpu.get_barrier_semaphore()
+
+    def greet(k, _):
+        pl.semaphore_signal(
+            barrier, inc=1, device_id=(chan, lax.rem(win + k, WIN)), device_id_type=MESH
+        )
+        return 0
+
+    lax.fori_loop(1, WIN, greet, 0)
+    for place in MATES:
+        pl.semaphore_signal(barrier, inc=1, device_id=(at(place), win), device_id_type=MESH)
+
     def whiten(q):
         def add(f, total):
             for p in range(2):
@@ -68,7 +68,7 @@
                 total = total + v * v
             return total
 
-        total = lax.fori_loop(0, FREQ, add, jnp.zeros((PW, CH), F32))
+        total = lax.fori_loop(0, FREQ, add, jnp.zeros((PW, CH), F32), unroll=8)
         rms = jnp.sqrt(total * (1.0 / (2 * FREQ)) + 1e-6)
         factor = mask[pl.ds(q * PW, PW), :].astype(F32) / rms
 
@@ -79,13 +79,14 @@
                     send_v[b * PARTS + q, dst, p] = (v * factor).astype(BF16)
             return 0
 
-        lax.fori_loop(0, WIN, scale, 0)
+        lax.fori_loop(0, WIN, scale, 0, unroll=4)
 
     mine = pl.ds(pl.multiple_of(win * PW, PW), PW)
 
     def spread(u):
         def one(k, _):
-            dst = lax.rem(win + k, WIN)
+            apart = WIN // 2 + lax.div(k + 1, 2) * (1 - 2 * lax.rem(k, 2))
+            dst = lax.rem(win + apart, WIN)
             pltpu.make_async_remote_copy(
                 src_ref=send_v.at[u, dst], dst_ref=g.at[0, u, :, mine, :],
                 send_sem=a_send.at[u], recv_sem=a_recv.at[u],
@@ -93,7 +94,7 @@
             ).start()
             return 0
 
-        lax.fori_loop(1, WIN, one, 0)
+        lax.fori_loop(0, WIN - 1, one, 0)
         g[0, u, :, mine, :] = send_v[u, win]
 
     def spread_all(u):
@@ -266,18 +267,19 @@
                 acc[group] = jnp.zeros_like(acc[group])
 
     def take(b):
-        for slot, place in enumerate(FOREIGN):
+        for slot in (3, 4, 0, 1, 9, 5, 6, 7, 8, 2):
+            place = FOREIGN[slot]
             remote(
                 res_recv.at[b, slot], res_recv.at[b, slot], s_send.at[b, slot], s_recv.at[b, slot], (0, 0)
             ).wait_recv()
             keep(b, place, res_recv[b, slot].astype(F32))
 
-    acc[...] = jnp.zeros_like(acc)
     loads[0].wait()
     loads[1].wait()
     whiten(0)
     pl.semaphore_wait(barrier, WIN - 1 + len(MATES))
     spread(0)
+    acc[...] = jnp.zeros_like(acc)
     for q in range(1, PARTS):
         loads[1 + q].wait()
         whiten(q)

time: 64.1 us -> 61.9 us (0.966)
  Pallas kernels: 61.5 us -> 59.5 us
    pallas_call x1, Pallas kernels: 61.5 us -> 59.5 us  [body(): pl.pallas_call(kernel, out_shape=pltpu.VMEM((BINS, 2, CH, CH * SIDE * SID...]
where the time goes in v4:
time: 61.9 us; the launch traced here: 61.5 us
  Pallas kernels  59.5 us (96%)
  local copies, waits for them, and re-layouts  2.02 us (3%)
    pallas_call x1, Pallas kernels, body(): pl.pallas_call(kernel, out_shape=pltpu.VMEM((BINS, 2, CH, CH * SIDE * SID...  59.5 us
    unnamed x1, local copies, waits for them, and re-layouts  2.02 us

profile of v4, /device:TPU:1, one launch (start us, length us, event | category | flops | bytes accessed | tf_op | source)
XLA Modules:
  0.0 61.5 jit_solution(15014521155880612558)
XLA Ops:
  0.0 59.5 %shard_map.28 = f32[2,2,128,2048]{3,2,1,0:T(8,128)S(1)} custom-call(f32[2,2048,128]{2,1,0:T(8,128)} %bitcast.1, s32[64,128]{1,0:T(8,128)} %mask_hbm.1), custom_call_target="tpu_custom_call" | custom-call | flops 5200000000 | bytes 6291456 | tf_op jit(solution)/shard_map/pallas_call | solution.py:371
  59.5 2.0 %copy.4 = f32[2,2,128,2048]{3,2,1,0:T(8,128)} copy(f32[2,2,128,2048]{3,2,1,0:T(8,128)S(1)} %shard_map.28) | data formatting | bytes 8388608

commit v5 on v4

--- a/solution.py
+++ b/solution.py
@@ -311,13 +311,13 @@
         def _():
             early(t - EARLY)
 
+        pl.when(t == UNITS)(lambda: send_early(1))
         pl.when(t == SEND_NEAR)(lambda: send_early(0))
 
         @pl.when(t == UNITS + 1)
         def _():
             for copy in relay(UNITS - 1):
                 copy.wait_send()
-            send_early(1)
 
         @pl.when(t == SEND_FAR)
         def _():

time: 61.9 us -> 61 us (0.985)
  no operation moved by 1% of the time
where the time goes in v5:
time: 61 us
  Pallas kernels  58.9 us (97%)
  local copies, waits for them, and re-layouts  2.02 us (3%)
    pallas_call x1, Pallas kernels, body(): pl.pallas_call(kernel, out_shape=pltpu.VMEM((BINS, 2, CH, CH * SIDE * SID...  58.9 us
    unnamed x1, local copies, waits for them, and re-layouts  2.02 us

profile of v5, /device:TPU:1, one launch (start us, length us, event | category | flops | bytes accessed | tf_op | source)
XLA Modules:
  0.0 61.0 jit_solution(6417628376871641823)
XLA Ops:
  0.0 58.9 %shard_map.28 = f32[2,2,128,2048]{3,2,1,0:T(8,128)S(1)} custom-call(f32[2,2048,128]{2,1,0:T(8,128)} %bitcast.1, s32[64,128]{1,0:T(8,128)} %mask_hbm.1), custom_call_target="tpu_custom_call" | custom-call | flops 5200000000 | bytes 6291456 | tf_op jit(solution)/shard_map/pallas_call | solution.py:371
  58.9 2.0 %copy.4 = f32[2,2,128,2048]{3,2,1,0:T(8,128)} copy(f32[2,2,128,2048]{3,2,1,0:T(8,128)S(1)} %shard_map.28) | data formatting | bytes 8388608

commit v6 on v5

--- a/solution.py
+++ b/solution.py
@@ -374,7 +374,7 @@
         in_specs=[pl.BlockSpec(memory_space=pltpu.HBM)] * 2,
         out_specs=pl.BlockSpec(memory_space=pltpu.VMEM),
         scratch_shapes=[
-            pltpu.VMEM((2, LW * FREQ, CH), F32),
+            pltpu.VMEM((2, LW * FREQ + FREQ, CH), F32),
             pltpu.VMEM((LW, CH), jnp.int32),
             pltpu.VMEM((UNITS, WIN, 2, PW, CH), BF16),
             pltpu.VMEM((len(PLACES), UNITS, 2, DEEP, CH), BF16),

time: 61 us -> 61 us (level)
  no operation moved by 1% of the time
where the time goes in v6:
time: 61 us
  Pallas kernels  58.9 us (97%)
  local copies, waits for them, and re-layouts  2.02 us (3%)
    pallas_call x1, Pallas kernels, body(): pl.pallas_call(kernel, out_shape=pltpu.VMEM((BINS, 2, CH, CH * SIDE * SID...  58.9 us
    unnamed x1, local copies, waits for them, and re-layouts  2.02 us

profile of v6, /device:TPU:1, one launch (start us, length us, event | category | flops | bytes accessed | tf_op | source)
XLA Modules:
  0.0 61.0 jit_solution(17106518720447232757)
XLA Ops:
  0.0 58.9 %shard_map.28 = f32[2,2,128,2048]{3,2,1,0:T(8,128)S(1)} custom-call(f32[2,2048,128]{2,1,0:T(8,128)} %bitcast.1, s32[64,128]{1,0:T(8,128)} %mask_hbm.1), custom_call_target="tpu_custom_call" | custom-call | flops 5200000000 | bytes 6291456 | tf_op jit(solution)/shard_map/pallas_call | solution.py:371
  58.9 2.0 %copy.4 = f32[2,2,128,2048]{3,2,1,0:T(8,128)} copy(f32[2,2,128,2048]{3,2,1,0:T(8,128)S(1)} %shard_map.28) | data formatting | bytes 8388608

commit v7 on v6

--- a/solution.py
+++ b/solution.py
@@ -17,7 +17,7 @@
 PARTS = 4
 PW = LW // PARTS
 AHEAD = 2
-EARLY, LATE = 1, 4
+EARLY, LATE = 1, 3
 SEND_NEAR, SEND_FAR = 9, 9
 UNITS = BINS * PARTS
 DEEP = WIN * PW
@@ -61,7 +61,7 @@
     for place in MATES:
         pl.semaphore_signal(barrier, inc=1, device_id=(at(place), win), device_id_type=MESH)
 
-    def whiten(q):
+    def level(q):
         def add(f, total):
             for p in range(2):
                 v = spec_v[p, pl.ds(q * ROWS + f, PW, stride=FREQ), :]
@@ -70,10 +70,11 @@
 
         total = lax.fori_loop(0, FREQ, add, jnp.zeros((PW, CH), F32), unroll=8)
         rms = jnp.sqrt(total * (1.0 / (2 * FREQ)) + 1e-6)
-        factor = mask[pl.ds(q * PW, PW), :].astype(F32) / rms
-
+        return mask[pl.ds(q * PW, PW), :].astype(F32) / rms
+
+    def whiten(q, factor, bins):
         def scale(dst, _):
-            for b in range(BINS):
+            for b in bins:
                 for p in range(2):
                     v = spec_v[p, pl.ds(q * ROWS + dst * BINS + b, PW, stride=FREQ), :]
                     send_v[b * PARTS + q, dst, p] = (v * factor).astype(BF16)
@@ -276,13 +277,15 @@
 
     loads[0].wait()
     loads[1].wait()
-    whiten(0)
+    first = level(0)
+    whiten(0, first, (0,))
     pl.semaphore_wait(barrier, WIN - 1 + len(MATES))
     spread(0)
+    whiten(0, first, range(1, BINS))
     acc[...] = jnp.zeros_like(acc)
     for q in range(1, PARTS):
         loads[1 + q].wait()
-        whiten(q)
+        whiten(q, level(q), range(BINS))
     for u in range(1, AHEAD):
         spread(u)
 

time: 61 us -> 60.9 us (level)
  no operation moved by 1% of the time
where the time goes in v7:
time: 60.9 us; the launch traced here: 60.8 us
  Pallas kernels  58.8 us (97%)
  local copies, waits for them, and re-layouts  2.02 us (3%)
    pallas_call x1, Pallas kernels, body(): pl.pallas_call(kernel, out_shape=pltpu.VMEM((BINS, 2, CH, CH * SIDE * SID...  58.8 us
    unnamed x1, local copies, waits for them, and re-layouts  2.02 us

profile of v7, /device:TPU:1, one launch (start us, length us, event | category | flops | bytes accessed | tf_op | source)
XLA Modules:
  0.0 60.8 jit_solution(4353373972052584721)
XLA Ops:
  0.0 58.8 %shard_map.28 = f32[2,2,128,2048]{3,2,1,0:T(8,128)S(1)} custom-call(f32[2,2048,128]{2,1,0:T(8,128)} %bitcast.1, s32[64,128]{1,0:T(8,128)} %mask_hbm.1), custom_call_target="tpu_custom_call" | custom-call | flops 5200000000 | bytes 6291456 | tf_op jit(solution)/shard_map/pallas_call | solution.py:374
  58.8 2.0 %copy.4 = f32[2,2,128,2048]{3,2,1,0:T(8,128)} copy(f32[2,2,128,2048]{3,2,1,0:T(8,128)S(1)} %shard_map.28) | data formatting | bytes 8388608
